TPU v7x, 256 devices: a whole 4x4x8 slice. The times are simulated.
256 devices in a mesh: sample: 4 (over y_lo, core), row: 16 (over z, y_hi), col: 4 (over x).
Axes of the slice: x: 4, y: 4 (y_hi: 2, y_lo: 2; y = y_hi * 2 + y_lo), z: 8, core: 2. Of those that a mesh axis runs over, the one named last changes fastest.
Arguments:
- trunk_pair: bfloat16 [1024, 1024, 128], P('row', 'col'), may hold values from -6 to 6
- distance_bins: int32 [4, 1024, 1024], P('sample', 'row', 'col'), may hold values from 0 to 38
- token_mask: int32 [1024], replicated, may hold values 0 or 1
- single: bfloat16 [1024, 384], P('row', 'sample'), may hold values from -6 to 6
- dist_weight: bfloat16 [39, 128], replicated, may hold values from -5 to 5
- pair_gain: float32 [128], replicated, may hold values from 0.1 to 1.9
- bias_weight: bfloat16 [128, 16], replicated
- single_gain: float32 [384], replicated, may hold values from 0.1 to 1.9
- query_weight: bfloat16 [384, 384], P(None, 'col'), may hold values from -0.3125 to 0.3125
- query_bias: float32 [384], P('col'), may hold values from -3 to 3
- key_weight: bfloat16 [384, 384], P(None, 'col'), may hold values from -0.3125 to 0.3125
- value_weight: bfloat16 [384, 384], P(None, 'col'), may hold values from -0.3125 to 0.3125
- gate_weight: bfloat16 [384, 384], P(None, 'col'), may hold values from -0.3125 to 0.3125
- out_weight: bfloat16 [384, 384], P('col'), may hold values from -0.3125 to 0.3125
Outputs:
- single_update: bfloat16 [4, 1024, 384], P('sample', 'row', 'col')
All inputs are finite; a program needn't handle non-finite values.
Results may differ from a plain program's by a relative error of at most 0.015.
The roundings to bfloat16 on the way count: a program that leaves them out, or rounds other values in their place, can miss the bound.
Values may be sent and summed in bfloat16 or wider, within the bound.
No kernel may reach another device: no remote copies, remote signals or barrier semaphores. Data moves between devices by JAX's collectives and lax.ppermute only.
A program may use at most 64 MiB of HBM per device.

v0:
```python
import jax
import jax.numpy as jnp
from jax import lax
from jax.sharding import PartitionSpec as P


def layer_norm(values, gain):
    mean = jnp.mean(values, axis=-1, keepdims=True)
    centered = values - mean
    var = jnp.mean(centered * centered, axis=-1, keepdims=True)
    return centered * lax.rsqrt(var + 1e-05) * gain


def attend_block(carry, q_heads, key_block, value_block, bias_part, mask_part):
    running_max, running_sum, running_acc = carry
    scale = 1.0 / jnp.sqrt(jnp.float32(q_heads.shape[2]))
    scores = (
        jnp.einsum("hqd,khd->hqk", q_heads, key_block, preferred_element_type=jnp.float32) * scale
    )
    scores = scores + bias_part.astype(jnp.float32)
    scores = scores + ((mask_part.astype(jnp.float32) - 1.0) * 1000000000.0)[None, None, :]
    new_max = jnp.maximum(running_max, jnp.max(scores, axis=-1))
    weights = jnp.exp(scores - new_max[..., None])
    new_sum = jnp.sum(weights, axis=-1)
    contrib = jnp.einsum(
        "hqk,khd->hqd",
        weights.astype(jnp.bfloat16),
        value_block,
        preferred_element_type=jnp.float32,
    )
    return (new_max, new_sum, contrib)


def body(
    trunk_pair,
    distance_bins,
    token_mask,
    single,
    dist_weight,
    pair_gain,
    bias_weight,
    single_gain,
    query_weight,
    query_bias,
    key_weight,
    value_weight,
    gate_weight,
    out_weight,
):
    heads_total = bias_weight.shape[1]
    channels = trunk_pair.shape[2]
    group_width = query_weight.shape[1]
    head_dim = single_gain.shape[0] // heads_total
    group_heads = group_width // head_dim
    tile_rows = trunk_pair.shape[0]
    tile_cols = trunk_pair.shape[1]
    whole_single = lax.all_gather(single, "sample", axis=1, tiled=True)
    single_normed = layer_norm(whole_single.astype(jnp.float32), single_gain).astype(jnp.bfloat16)
    queries = (
        jnp.dot(single_normed, query_weight, preferred_element_type=jnp.float32) + query_bias
    ).astype(jnp.bfloat16)
    gate = jax.nn.sigmoid(jnp.dot(single_normed, gate_weight, preferred_element_type=jnp.float32))
    key_value_weight = jnp.concatenate([key_weight, value_weight], axis=1)
    padded_table = jnp.concatenate(
        [dist_weight, jnp.zeros((128 - dist_weight.shape[0], channels), jnp.bfloat16)], axis=0
    )
    onehot = (distance_bins[0][..., None] == jnp.arange(128, dtype=jnp.int32)).astype(jnp.bfloat16)
    embedded = jnp.dot(onehot.reshape(-1, 128), padded_table, preferred_element_type=jnp.float32)
    pair_s = trunk_pair.reshape(-1, channels).astype(jnp.float32) + embedded
    pair_normed = layer_norm(pair_s, pair_gain).astype(jnp.bfloat16)
    bias_tile = lax.dot_general(
        bias_weight, pair_normed, (((0,), (1,)), ((), ())), preferred_element_type=jnp.float32
    )
    bias_tile = bias_tile.astype(jnp.bfloat16).reshape(heads_total, tile_rows, tile_cols)
    q_heads = jnp.transpose(queries.reshape(tile_rows, group_heads, head_dim), (1, 0, 2))
    bias_heads = lax.all_to_all(bias_tile, "col", split_axis=0, concat_axis=2, tiled=True)
    start_carry = (
        jnp.full((group_heads, tile_rows), -1e30, jnp.float32),
        jnp.zeros((group_heads, tile_rows), jnp.float32),
        jnp.zeros((group_heads, tile_rows, head_dim), jnp.float32),
    )
    piece = lax.all_gather(single_normed, "row", axis=0, tiled=True)
    count = piece.shape[0]
    projected = jnp.dot(piece, key_value_weight, preferred_element_type=jnp.float32).astype(
        jnp.bfloat16
    )
    key_block = projected[:, :group_width].reshape(count, group_heads, head_dim)
    value_block = projected[:, group_width:].reshape(count, group_heads, head_dim)
    final_max, final_sum, final_acc = attend_block(
        start_carry, q_heads, key_block, value_block, bias_heads, token_mask
    )
    attended = final_acc / final_sum[..., None]
    attended = jnp.transpose(attended, (1, 0, 2)).reshape(tile_rows, group_width)
    gated = (gate * attended).astype(jnp.bfloat16)
    partial_update = jnp.dot(gated, out_weight, preferred_element_type=jnp.float32)
    update = lax.psum_scatter(partial_update, "col", scatter_dimension=1, tiled=True)
    return update.astype(jnp.bfloat16)[None]


def solution(mesh):
    placed = (
        P("row", "col", None),
        P("sample", "row", "col"),
        P(),
        P("row", "sample"),
        P(),
        P(),
        P(),
        P(),
        P(None, "col"),
        P("col"),
        P(None, "col"),
        P(None, "col"),
        P(None, "col"),
        P("col", None),
    )
    return jax.shard_map(
        body, mesh=mesh, in_specs=placed, out_specs=P("sample", "row", "col"), check_vma=False
    )
```

profile of v0, /device:TPU:8, one launch (start us, length us, event | category | flops | bytes accessed | tf_op | source)
XLA Modules:
  0.0 121.4 jit_solution(10705247466023171844)
XLA Ops:
  6.5 5.1 %bitcast_convert_fusion = f32[16384,128]{1,0:T(8,128)} fusion(bf16[64,256,128]{2,1,0:T(8,128)(2,1)} %param.14), kind=kLoop, calls=%fused_computation.5 | loop fusion | flops 2097152 | bytes 12582912 | tf_op jit(solution)/shard_map/convert_element_type | solution.py:69
  11.7 9.1 %copy.31 = f32[16384,128]{0,1:T(8,128)} copy(f32[16384,128]{1,0:T(8,128)} %bitcast_convert_fusion) | data formatting | bytes 16777216 | tf_op jit(solution)/shard_map/convert_element_type | solution.py:69
  20.8 7.9 %fusion.26 = (f32[16384]{0:T(1024)S(1)}, f32[16384,128]{0,1:T(8,128)S(1)}) fusion(f32[16384,128]{0,1:T(8,128)} %copy.31, bf16[39,128]{1,0:T(8,128)(2,1)S(1)} %copy-done.7, s32[16384]{0:T(1024)S(1)} %bitcast.53), kind=kOutput, calls=%fused_computation.49 | convolution fusion | flops 543145984 | bytes 16918272 | tf_op jit(solution)/shard_map/dot_general | solution.py:68
  28.7 0.0 copy-start.8
  28.7 0.0 copy-start.11
  28.8 1.0 multiply_reduce_fusion
  29.8 0.0 copy-start.12
  29.8 0.0 copy-start.3
  29.9 1.1 convolution_convert_fusion
  31.0 0.9 copy.36
  31.9 4.3 %all-to-all-start = ((bf16[16,64,256]{2,1,0:T(8,128)(2,1)}), bf16[16,64,256]{2,1,0:T(8,128)(2,1)S(1)}, u32[]{:S(2)}, u32[]{:S(2)}) async-start(bf16[16,64,256]{2,1,0:T(8,128)(2,1)} %bitcast.27), calls=%async_computation | async-start | bytes 1048576 | tf_op jit(solution)/shard_map/all_to_all | solution.py:76
  36.2 5.2 %all-gather = bf16[4,96,64]{1,2,0:T(8,128)(2,1)S(1)} all-gather(bf16[1,96,64]{1,2,0:T(8,128)(2,1)S(1)} %bitcast.58), channel_id=1, replica_groups=mesh['sample'=4,'row'=16,'col'=4] {'sample'}, dimensions={0}, use_global_device_ids=true | all-gather | bytes 61440 | tf_op jit(solution)/shard_map/all_gather | solution.py:57
  41.4 0.1 copy.26
  41.5 0.1 convert_reduce_fusion
  41.6 0.1 reshape.68
  41.8 0.2 multiply_reduce_fusion.1
  42.0 0.1 bitcast_convert_fusion.1
  42.0 47.7 %all_gather.7 = bf16[1024,384]{1,0:T(8,128)(2,1)S(1)} all-gather(bf16[64,384]{1,0:T(8,128)(2,1)S(1)} %bitcast_convert_fusion.1), channel_id=1, replica_groups=mesh['sample'=4,'row'=16,'col'=4] {'row'}, dimensions={0}, use_global_device_ids=true | all-gather | bytes 835584 | tf_op jit(solution)/shard_map/all_gather | solution.py:82
  89.8 0.2 fusion.12
  90.0 0.1 copy.27
  90.1 0.4 convolution_convert_fusion.1
  90.6 0.1 convert_bitcast_fusion
  90.7 0.1 copy.34
  90.8 0.4 fusion.27
  91.3 0.3 fusion.13
  91.6 0.3 fusion.6
  92.0 0.1 copy.30
  92.0 0.0 copy-done
  92.1 1.0 convolution_bitcast_fusion
  93.1 0.0 reduce-scatter.4.cloned.1.call-update
  93.1 19.9 %reduce-scatter.4.cloned.1.call-done = f32[96,64]{1,0:T(8,128)} async-done(((f32[384,64]{1,0:T(8,128)}), f32[96,64]{1,0:T(8,128)}) %reduce-scatter.4.cloned.1.call-update) | async-done | bytes 24592
  113.0 1.5 %copy.33 = bf16[64,96]{1,0:T(8,128)(2,1)} copy(f32[64,96]{0,1:T(8,128)} %bitcast.57) | data formatting | bytes 36864
  (31 shorter events, 0.2 us)
Async XLA Ops:
  6.5 85.5 %copy-start = (bf16[96,384]{1,0:T(8,128)(2,1)S(1)}, bf16[96,384]{1,0:T(8,128)(2,1)}, u32[]{:S(2)}) copy-start(bf16[96,384]{1,0:T(8,128)(2,1)} %param.27) | copy-start | bytes 221188
  11.7 9.1 %copy-start.5 = (s32[1,64,256]{2,1,0:T(8,128)S(1)}, s32[1,64,256]{2,1,0:T(8,128)}, u32[]{:S(2)}) copy-start(s32[1,64,256]{2,1,0:T(8,128)} %param.15) | copy-start | bytes 196612
  11.7 9.1 %copy-start.7 = (bf16[39,128]{1,0:T(8,128)(2,1)S(1)}, bf16[39,128]{1,0:T(8,128)(2,1)}, u32[]{:S(2)}) copy-start(bf16[39,128]{1,0:T(8,128)(2,1)} %param.18) | copy-start | bytes 29956
  28.7 1.1 copy-start.8
  28.7 1.1 copy-start.11
  28.8 7.4 %copy-start.6 = (bf16[64,96]{1,0:T(8,128)(2,1)S(1)}, bf16[64,96]{1,0:T(8,128)(2,1)}, u32[]{:S(2)}) copy-start(bf16[64,96]{1,0:T(8,128)(2,1)} %param.17) | copy-start | bytes 36868
  28.8 13.2 %copy-start.10 = (f32[384]{0:T(512)S(1)}, f32[384]{0:T(512)}, u32[]{:S(2)}) copy-start(f32[384]{0:T(512)} %param.21) | copy-start | bytes 4612
  29.8 60.0 %copy-start.1 = (bf16[384,96]{0,1:T(8,128)(2,1)S(1)}, bf16[384,96]{0,1:T(8,128)(2,1)}, u32[]{:S(2)}) copy-start(bf16[384,96]{0,1:T(8,128)(2,1)} %param.22) | copy-start | bytes 221188
  29.8 60.0 %copy-start.12 = (f32[96]{0:T(128)S(1)}, f32[96]{0:T(128)}, u32[]{:S(2)}) copy-start(f32[96]{0:T(128)} %param.23) | copy-start | bytes 1156
  29.8 60.3 %copy-start.3 = (bf16[384,96]{0,1:T(8,128)(2,1)S(1)}, bf16[384,96]{0,1:T(8,128)(2,1)}, u32[]{:S(2)}) copy-start(bf16[384,96]{0,1:T(8,128)(2,1)} %param.25) | copy-start | bytes 221188
  29.8 60.3 %copy-start.4 = (bf16[384,96]{0,1:T(8,128)(2,1)S(1)}, bf16[384,96]{0,1:T(8,128)(2,1)}, u32[]{:S(2)}) copy-start(bf16[384,96]{0,1:T(8,128)(2,1)} %param.24) | copy-start | bytes 221188
  29.8 60.7 %copy-start.9 = (s32[1024]{0:T(1024)S(1)}, s32[1024]{0:T(1024)}, u32[]{:S(2)}) copy-start(s32[1024]{0:T(1024)} %param.16) | copy-start | bytes 12292
  31.0 61.1 %copy-start.2 = (bf16[384,96]{0,1:T(8,128)(2,1)S(1)}, bf16[384,96]{0,1:T(8,128)(2,1)}, u32[]{:S(2)}) copy-start(bf16[384,96]{0,1:T(8,128)(2,1)} %param.26) | copy-start | bytes 221188
  31.9 58.7 %all-to-all-start = ((bf16[16,64,256]{2,1,0:T(8,128)(2,1)}), bf16[16,64,256]{2,1,0:T(8,128)(2,1)S(1)}, u32[]{:S(2)}, u32[]{:S(2)}) async-start(bf16[16,64,256]{2,1,0:T(8,128)(2,1)} %bitcast.27), calls=%async_computation | async-start | bytes 1048576 | tf_op jit(solution)/shard_map/all_to_all | solution.py:76
  36.2 76.8 %reduce-scatter.4.cloned.1.call-start = ((), (), s32[]{:S(2)}) async-start(), calls=%async_computation.2 | async-start | bytes 245760
Sparse Core Ops, SparseCore 0:
  93.2 19.7 reduce-scatter.3
where the time goes:
time: 122 us; the launch traced here: 121 us
  blocking collectives  53 us (43%)
  waiting for transfers between devices  19.9 us (16%)
  between operations  13.7 us (11%)
  local copies, waits for them, and re-layouts  12.1 us (10%)
  matrix products  11.5 us (9%)
  other arithmetic  6.93 us (6%)
  starting transfers between devices  4.29 us (4%)
    all_gather x1, blocking collectives, body(): piece = lax.all_gather(single_normed, 'row', axis=0, tiled=True)  47.7 us
    unnamed x2, waiting for transfers between devices  19.9 us
    convert_element_type x1, local copies, waits for them, and re-layouts, body(): pair_s = trunk_pair.reshape(-1, channels).astype(jnp.float32) + embedded  9.08 us
    dot_general x1, matrix products, body(): jnp.dot(onehot.reshape(-1, 128), padded_table, preferred_element_type=jnp...  7.93 us
    all_gather x1, blocking collectives, body(): whole_single = lax.all_gather(single, 'sample', axis=1, tiled=True)  5.24 us
    convert_element_type x1, other arithmetic, body(): pair_s = trunk_pair.reshape(-1, channels).astype(jnp.float32) + embedded  5.11 us
    all_to_all x1, starting transfers between devices, body(): lax.all_to_all(bias_tile, 'col', split_axis=0, concat_axis=2, tiled=True)  4.29 us
    unnamed x29, local copies, waits for them, and re-layouts  2.51 us
  transfers between devices with their start and end apart: 2, of which 1 were waited for; matrix products, arithmetic and copies ran while one was open for 1% of the time, Pallas kernels for 0%

commit v1 on v0

--- a/solution.py
+++ b/solution.py
@@ -79,7 +79,15 @@
         jnp.zeros((group_heads, tile_rows), jnp.float32),
         jnp.zeros((group_heads, tile_rows, head_dim), jnp.float32),
     )
-    piece = lax.all_gather(single_normed, "row", axis=0, tiled=True)
+    piece = jnp.concatenate(
+        lax.all_to_all(
+            jnp.stack(lax.axis_size("row") * [single_normed]),
+            axis_name="row",
+            split_axis=0,
+            concat_axis=0,
+        ),
+        axis=0,
+    )
     count = piece.shape[0]
     projected = jnp.dot(piece, key_value_weight, preferred_element_type=jnp.float32).astype(
         jnp.bfloat16

time: 122 us -> 109 us (0.89)
  blocking collectives: 53 us -> 5.23 us
  waiting for transfers between devices: 19.9 us -> 43.7 us
  starting transfers between devices: 4.29 us -> 14.6 us
    all_gather x1 -> x0, blocking collectives: 47.7 us -> none  [body(): piece = lax.all_gather(single_normed, 'row', axis=0, tiled=True)]
    all_to_all x0 -> x1, waiting for transfers between devices: none -> 22 us  [body(): lax.all_to_all(jnp.stack(lax.axis_size('row') * [single_normed]), axis_na...]
    all_to_all x0 -> x1, starting transfers between devices: none -> 10.3 us  [body(): lax.all_to_all(jnp.stack(lax.axis_size('row') * [single_normed]), axis_na...]
    all_to_all x1, waiting for transfers between devices: 0.01 us -> 3.64 us  [body(): lax.all_to_all(bias_tile, 'col', split_axis=0, concat_axis=2, tiled=True)]
    unnamed x2, waiting for transfers between devices: 19.9 us -> 18.1 us
  transfers between devices with their start and end apart: 2 -> 3, of which waited for: 1 -> 3; matrix products, arithmetic and copies ran while one was open for 1% -> 1% of each run, Pallas kernels for 0% -> 0%
where the time goes in v1:
time: 109 us
  waiting for transfers between devices  43.7 us (40%)
  starting transfers between devices  14.6 us (13%)
  between operations  13.7 us (13%)
  local copies, waits for them, and re-layouts  13.1 us (12%)
  matrix products  11.4 us (10%)
  other arithmetic  6.94 us (6%)
  blocking collectives  5.23 us (5%)
    all_to_all x1, waiting for transfers between devices, body(): lax.all_to_all(jnp.stack(lax.axis_size('row') * [single_normed]), axis_na...  22 us
    unnamed x2, waiting for transfers between devices  18.1 us
    all_to_all x1, starting transfers between devices, body(): lax.all_to_all(jnp.stack(lax.axis_size('row') * [single_normed]), axis_na...  10.3 us
    convert_element_type x1, local copies, waits for them, and re-layouts, body(): pair_s = trunk_pair.reshape(-1, channels).astype(jnp.float32) + embedded  9.02 us
    dot_general x1, matrix products, body(): jnp.dot(onehot.reshape(-1, 128), padded_table, preferred_element_type=jnp...  7.93 us
    all_gather x1, blocking collectives, body(): whole_single = lax.all_gather(single, 'sample', axis=1, tiled=True)  5.23 us
    convert_element_type x1, other arithmetic, body(): pair_s = trunk_pair.reshape(-1, channels).astype(jnp.float32) + embedded  5.12 us
    all_to_all x1, starting transfers between devices, body(): lax.all_to_all(bias_tile, 'col', split_axis=0, concat_axis=2, tiled=True)  4.29 us
  transfers between devices with their start and end apart: 3, of which 3 were waited for; matrix products, arithmetic and copies ran while one was open for 1% of the time, Pallas kernels for 0%

profile of v1, /device:TPU:8, one launch (start us, length us, event | category | flops | bytes accessed | tf_op | source)
XLA Modules:
  0.0 108.6 jit_solution(14331651830527900083)
XLA Ops:
  6.5 5.1 %bitcast_convert_fusion = f32[16384,128]{1,0:T(8,128)} fusion(bf16[64,256,128]{2,1,0:T(8,128)(2,1)} %param.14), kind=kLoop, calls=%fused_computation.5 | loop fusion | flops 2097152 | bytes 12582912 | tf_op jit(solution)/shard_map/convert_element_type | solution.py:69
  11.7 9.0 %copy.32 = f32[16384,128]{0,1:T(8,128)} copy(f32[16384,128]{1,0:T(8,128)} %bitcast_convert_fusion) | data formatting | bytes 16777216 | tf_op jit(solution)/shard_map/convert_element_type | solution.py:69
  20.7 7.9 %fusion.26 = (f32[16384]{0:T(1024)S(1)}, f32[16384,128]{0,1:T(8,128)S(1)}) fusion(f32[16384,128]{0,1:T(8,128)} %copy.32, bf16[39,128]{1,0:T(8,128)(2,1)S(1)} %copy-done.7, s32[16384]{0:T(1024)S(1)} %bitcast.55), kind=kOutput, calls=%fused_computation.49 | convolution fusion | flops 543145984 | bytes 16918272 | tf_op jit(solution)/shard_map/dot_general | solution.py:68
  28.7 1.0 multiply_reduce_fusion
  29.8 1.1 %convolution_convert_fusion = bf16[16384,16]{0,1:T(8,128)(2,1)S(1)} fusion(bf16[128,16]{0,1:T(8,128)(2,1)S(1)} %copy-done.8, f32[16384,128]{0,1:T(8,128)S(1)} %get-tuple-element.8, f32[128]{0:T(128)S(1)} %copy-done.11, f32[16384]{0:T(1024)S(1)} %add_rsqrt_fusion, f32[16384]{0:T(1024)S(1)} %broadcast_multiply_fusion), kind=kOutput, calls=%fused_computation.1 | convolution fusion | flops 75759616 | bytes 9048576 | tf_op jit(solution)/shard_map/dot_general | solution.py:71
  31.0 0.9 copy.37
  31.9 4.3 %all-to-all-start.1 = ((bf16[16,64,256]{2,1,0:T(8,128)(2,1)}), bf16[16,64,256]{2,1,0:T(8,128)(2,1)S(1)}, u32[]{:S(2)}, u32[]{:S(2)}) async-start(bf16[16,64,256]{2,1,0:T(8,128)(2,1)} %bitcast.28), calls=%async_computation.1 | async-start | bytes 1048576 | tf_op jit(solution)/shard_map/all_to_all | solution.py:76
  36.2 5.2 %all-gather = bf16[4,96,64]{1,2,0:T(8,128)(2,1)S(1)} all-gather(bf16[1,96,64]{1,2,0:T(8,128)(2,1)S(1)} %bitcast.60), channel_id=1, replica_groups=mesh['sample'=4,'row'=16,'col'=4] {'sample'}, dimensions={0}, use_global_device_ids=true | all-gather | bytes 61440 | tf_op jit(solution)/shard_map/all_gather | solution.py:57
  41.4 0.1 copy.27
  41.4 0.1 convert_reduce_fusion
  41.6 0.1 reshape.74
  41.7 0.2 multiply_reduce_fusion.1
  41.9 0.1 bitcast_convert_fusion.1
  42.0 3.6 %all-to-all-done.1 = bf16[16,64,256]{2,1,0:T(8,128)(2,1)S(1)} async-done(((bf16[16,64,256]{2,1,0:T(8,128)(2,1)}), bf16[16,64,256]{2,1,0:T(8,128)(2,1)S(1)}, u32[]{:S(2)}, u32[]{:S(2)}) %all-to-all-start.1) | async-done | bytes 524320 | tf_op jit(solution)/shard_map/all_to_all | solution.py:76
  45.6 1.0 stack.2
  46.6 10.3 %all-to-all-start = ((bf16[16,64,384]{2,1,0:T(8,128)(2,1)}), bf16[16,64,384]{2,1,0:T(8,128)(2,1)S(1)}, u32[]{:S(2)}, u32[]{:S(2)}) async-start(bf16[16,64,384]{2,1,0:T(8,128)(2,1)} %stack.2), calls=%async_computation | async-start | bytes 1572864 | tf_op jit(solution)/shard_map/all_to_all | solution.py:83
  56.9 0.0 reduce-scatter.4.cloned.1.call-start
  57.0 0.2 fusion.12
  57.2 0.1 copy.28
  57.3 0.1 convert_bitcast_fusion
  57.4 0.1 copy.35
  57.6 22.0 %all-to-all-done = bf16[16,64,384]{2,1,0:T(8,128)(2,1)S(1)} async-done(((bf16[16,64,384]{2,1,0:T(8,128)(2,1)}), bf16[16,64,384]{2,1,0:T(8,128)(2,1)S(1)}, u32[]{:S(2)}, u32[]{:S(2)}) %all-to-all-start) | async-done | bytes 786464 | tf_op jit(solution)/shard_map/all_to_all | solution.py:83
  79.5 0.4 convolution_convert_fusion.1
  80.0 0.4 fusion.27
  80.4 0.3 fusion.13
  80.8 0.3 fusion.6
  81.1 0.1 copy.31
  81.2 0.0 copy-done
  81.2 1.0 convolution_bitcast_fusion
  82.2 0.0 reduce-scatter.4.cloned.1.call-update
  82.3 18.0 %reduce-scatter.4.cloned.1.call-done = f32[96,64]{1,0:T(8,128)} async-done(((f32[384,64]{1,0:T(8,128)}), f32[96,64]{1,0:T(8,128)}) %reduce-scatter.4.cloned.1.call-update) | async-done | bytes 24592
  100.3 1.5 %copy.34 = bf16[64,96]{1,0:T(8,128)(2,1)} copy(f32[64,96]{0,1:T(8,128)} %bitcast.59) | data formatting | bytes 36864
  (33 shorter events, 0.2 us)
Async XLA Ops:
  6.5 74.7 %copy-start = (bf16[96,384]{1,0:T(8,128)(2,1)S(1)}, bf16[96,384]{1,0:T(8,128)(2,1)}, u32[]{:S(2)}) copy-start(bf16[96,384]{1,0:T(8,128)(2,1)} %param.27) | copy-start | bytes 221188
  11.7 9.0 %copy-start.5 = (s32[1,64,256]{2,1,0:T(8,128)S(1)}, s32[1,64,256]{2,1,0:T(8,128)}, u32[]{:S(2)}) copy-start(s32[1,64,256]{2,1,0:T(8,128)} %param.15) | copy-start | bytes 196612
  11.7 9.1 %copy-start.7 = (bf16[39,128]{1,0:T(8,128)(2,1)S(1)}, bf16[39,128]{1,0:T(8,128)(2,1)}, u32[]{:S(2)}) copy-start(bf16[39,128]{1,0:T(8,128)(2,1)} %param.18) | copy-start | bytes 29956
  28.7 1.1 %copy-start.8 = (bf16[128,16]{0,1:T(8,128)(2,1)S(1)}, bf16[128,16]{0,1:T(8,128)(2,1)}, u32[]{:S(2)}) copy-start(bf16[128,16]{0,1:T(8,128)(2,1)} %param.20) | copy-start | bytes 12292
  28.7 1.1 %copy-start.11 = (f32[128]{0:T(128)S(1)}, f32[128]{0:T(128)}, u32[]{:S(2)}) copy-start(f32[128]{0:T(128)} %param.19) | copy-start | bytes 1540
  28.7 7.4 %copy-start.6 = (bf16[64,96]{1,0:T(8,128)(2,1)S(1)}, bf16[64,96]{1,0:T(8,128)(2,1)}, u32[]{:S(2)}) copy-start(bf16[64,96]{1,0:T(8,128)(2,1)} %param.17) | copy-start | bytes 36868
  28.7 13.2 %copy-start.10 = (f32[384]{0:T(512)S(1)}, f32[384]{0:T(512)}, u32[]{:S(2)}) copy-start(f32[384]{0:T(512)} %param.21) | copy-start | bytes 4612
  29.7 27.3 %copy-start.1 = (bf16[384,96]{0,1:T(8,128)(2,1)S(1)}, bf16[384,96]{0,1:T(8,128)(2,1)}, u32[]{:S(2)}) copy-start(bf16[384,96]{0,1:T(8,128)(2,1)} %param.22) | copy-start | bytes 221188
  29.7 27.3 %copy-start.12 = (f32[96]{0:T(128)S(1)}, f32[96]{0:T(128)}, u32[]{:S(2)}) copy-start(f32[96]{0:T(128)} %param.23) | copy-start | bytes 1156
  29.7 27.6 %copy-start.9 = (s32[1024]{0:T(1024)S(1)}, s32[1024]{0:T(1024)}, u32[]{:S(2)}) copy-start(s32[1024]{0:T(1024)} %param.16) | copy-start | bytes 12292
  29.8 49.7 %copy-start.3 = (bf16[384,96]{0,1:T(8,128)(2,1)S(1)}, bf16[384,96]{0,1:T(8,128)(2,1)}, u32[]{:S(2)}) copy-start(bf16[384,96]{0,1:T(8,128)(2,1)} %param.25) | copy-start | bytes 221188
  29.8 49.7 %copy-start.4 = (bf16[384,96]{0,1:T(8,128)(2,1)S(1)}, bf16[384,96]{0,1:T(8,128)(2,1)}, u32[]{:S(2)}) copy-start(bf16[384,96]{0,1:T(8,128)(2,1)} %param.24) | copy-start | bytes 221188
  30.9 50.2 %copy-start.2 = (bf16[384,96]{0,1:T(8,128)(2,1)S(1)}, bf16[384,96]{0,1:T(8,128)(2,1)}, u32[]{:S(2)}) copy-start(bf16[384,96]{0,1:T(8,128)(2,1)} %param.26) | copy-start | bytes 221188
  31.9 13.8 %all-to-all-start.1 = ((bf16[16,64,256]{2,1,0:T(8,128)(2,1)}), bf16[16,64,256]{2,1,0:T(8,128)(2,1)S(1)}, u32[]{:S(2)}, u32[]{:S(2)}) async-start(bf16[16,64,256]{2,1,0:T(8,128)(2,1)} %bitcast.28), calls=%async_computation.1 | async-start | bytes 1048576 | tf_op jit(solution)/shard_map/all_to_all | solution.py:76
  46.6 32.9 %all-to-all-start = ((bf16[16,64,384]{2,1,0:T(8,128)(2,1)}), bf16[16,64,384]{2,1,0:T(8,128)(2,1)S(1)}, u32[]{:S(2)}, u32[]{:S(2)}) async-start(bf16[16,64,384]{2,1,0:T(8,128)(2,1)} %stack.2), calls=%async_computation | async-start | bytes 1572864 | tf_op jit(solution)/shard_map/all_to_all | solution.py:83
  56.9 43.4 %reduce-scatter.4.cloned.1.call-start = ((), (), s32[]{:S(2)}) async-start(), calls=%async_computation.3 | async-start | bytes 245760
Sparse Core Ops, SparseCore 0:
  82.4 17.8 reduce-scatter.3
